TPU v7x, 32 devices: a whole 2x2x4 slice. The times are simulated.
32 devices in a mesh: lst: 4 (over y, x), night: 8 (over z, core).
Axes of the slice: x: 2, y: 2, z: 4, core: 2. Of those that a mesh axis runs over, the one named last changes fastest.
Arguments:
- visibility: bfloat16 [8, 32, 16, 2, 1536], P('night', 'lst'), may hold values from -18 to 18
- flags: int32 [8, 32, 16, 1536], P('night', 'lst'), may hold values 0 or 1
- counts: int32 [8, 32], P('night', 'lst'), may hold values from 1 to 4
- offsets: int32 [8], P('night'), may hold values from -6 to 6, as said below
- fraction: float32 [8], P('night'), may hold values from 0 to 1
- gains: float32 [8, 2, 1536], P('night'), may hold values from -6 to 6
- inverse_var: float32 [8, 1536], P('night'), may hold values from 0.005 to 0.05
- prior: float32 [1536], replicated, may hold values from 0.5 to 5
Outputs:
- binned: bfloat16 [32, 16, 2, 1536], P('lst')
- weight_total: float32 [32, 16, 1536], P('lst')
Inputs may be any that keep to these rules, and one draw needn't show every extreme that they name: `offsets`: both -6 and 6 occur among the nights.
All inputs are finite; a program needn't handle non-finite values. No bound on the sum of `flags` on one device may be relied on, other than what follows from the above.
Results may differ from a plain program's by a relative error of at most 0.009.
Values may be sent and summed in bfloat16 or wider, within the bound.
A program may use at most 64 MiB of HBM per device.

v0:
```python
import jax
import jax.numpy as jnp
from jax import lax
from jax.sharding import PartitionSpec as P


def extended(x, sides, width):
    for axis, dim in sides:
        size, length = (lax.axis_size(axis), x.shape[dim])
        up = [(i, (i + 1) % size) for i in range(size)]
        down = [(j, i) for i, j in up]
        last = lax.slice_in_dim(x, length - width, length, axis=dim)
        first = lax.slice_in_dim(x, 0, width, axis=dim)
        before = lax.ppermute(last, axis, up)
        after = lax.ppermute(first, axis, down)
        x = jnp.concatenate([before, x, after], axis=dim)
    return x


def spline_taps(fraction):
    cube = fraction * fraction * fraction
    square = fraction * fraction
    first = (1.0 - fraction) ** 3 / 6.0
    second = (3.0 * cube - 6.0 * square + 4.0) / 6.0
    third = (-3.0 * cube + 3.0 * square + 3.0 * fraction + 1.0) / 6.0
    fourth = cube / 6.0
    return jnp.stack([first, second, third, fourth], axis=-1)


def shards(visibility, flags, counts, offsets, fraction, gains, inverse_var, prior):
    local_nights = visibility.shape[0]
    sample_count = visibility.shape[1]
    baseline_count = visibility.shape[2]
    channel_count = visibility.shape[4]
    scale = (flags * counts[:, :, None, None]).astype(jnp.float32) * inverse_var[:, None, None, :]
    weight = scale.astype(jnp.bfloat16)
    real_part = visibility[:, :, :, 0].astype(jnp.float32)
    imag_part = visibility[:, :, :, 1].astype(jnp.float32)
    gain_re = gains[:, 0][:, None, None, :]
    gain_im = gains[:, 1][:, None, None, :]
    cal_re = gain_re * real_part - gain_im * imag_part
    cal_im = gain_re * imag_part + gain_im * real_part
    weighted = (scale[:, :, :, None, :] * jnp.stack([cal_re, cal_im], axis=3)).astype(jnp.bfloat16)
    stacked = jnp.concatenate([weighted, weight[:, :, :, None, :]], axis=3)
    taps = spline_taps(fraction)
    tap_index = jnp.arange(4).reshape(1, 1, 1, 4)
    shifts = offsets.reshape(1, local_nights, 1, 1)
    tap_values = taps.reshape(1, local_nights, 1, 4)
    padded_slab = extended(stacked, (("lst", 1),), sample_count)
    out_row = jnp.arange(sample_count).reshape(sample_count, 1, 1, 1)
    source = jnp.arange(3 * sample_count).reshape(1, 1, 3 * sample_count, 1)
    target = out_row - shifts + tap_index - 1 + sample_count
    matrix = jnp.sum(jnp.where(source == target, tap_values, 0.0), axis=-1).astype(jnp.bfloat16)
    partial_numerator = jnp.dot(
        matrix.reshape(sample_count, local_nights * 3 * sample_count),
        padded_slab.reshape(local_nights * 3 * sample_count, baseline_count * 3 * channel_count),
        preferred_element_type=jnp.float32,
    )
    partial_numerator = partial_numerator.reshape(sample_count, baseline_count, 3, channel_count)
    totals = lax.psum(partial_numerator, "night")
    denominator_sum = totals[:, :, 2]
    binned = (
        totals[:, :, 0:2] / (denominator_sum[:, :, None, :] + prior[None, None, None, :])
    ).astype(jnp.bfloat16)
    return (binned, denominator_sum)


def solution(mesh):
    in_specs = (
        P("night", "lst", None, None, None),
        P("night", "lst", None, None),
        P("night", "lst"),
        P("night"),
        P("night"),
        P("night", None, None),
        P("night", None),
        P(),
    )
    out_specs = (P("lst", None, None, None), P("lst", None, None))
    return jax.shard_map(shards, mesh=mesh, in_specs=in_specs, out_specs=out_specs, check_vma=False)
```

profile of v0, /device:TPU:0, one launch (start us, length us, event | category | flops | bytes accessed | tf_op | source)
XLA Modules:
  0.0 172.8 jit_solution(5491326670959882846)
XLA Ops:
  7.2 0.0 copy-start.3
  7.2 0.0 copy-start.1
  7.2 0.0 copy-start.4
  7.2 0.0 all-reduce.2.cloned.1.call-start
  7.2 0.8 slice_reduce_fusion.1
  8.1 3.0 %fusion.11 = (bf16[1,8,16,1,1536]{4,3,2,1,0:T(2,128)(2,1)S(1)}, bf16[1,8,16,1,1536]{4,3,2,1,0:T(2,128)(2,1)S(1)}) fusion(bf16[1,8,16,2,1536]{4,3,2,1,0:T(2,128)(2,1)} %param.8), kind=kLoop, calls=%fused_computation.29 | loop fusion | bytes 1572864 | tf_op jit(solution)/shard_map/slice | solution.py:37
  11.1 0.0 copy-done.3
  11.2 0.0 copy-done.1
  11.2 0.0 copy-done.4
  11.2 0.2 fusion.7
  11.4 0.3 fusion.4
  11.7 0.1 fusion.3
  11.8 0.1 pad_maximum_fusion.1
  11.9 3.9 %collective-permute-start.1 = (bf16[1,8,16,3,1536]{4,2,3,1,0:T(8,128)(2,1)S(1)}, bf16[1,8,16,3,1536]{4,2,3,1,0:T(8,128)(2,1)S(1)}, u32[]{:S(2)}, u32[]{:S(2)}) collective-permute-start(bf16[1,8,16,3,1536]{4,2,3,1,0:T(8,128)(2,1)S(1)} %pad_maximum_fusion.1), channel_id=1, source_target_pairs={{8,0},{16,8},{24,16},{0,24},{9,1},{17,9},{25,17},{1,25},{10,2},{18... | collective-permute-start | bytes 3538952 | tf_op jit(solution)/shard_map/ppermute | solution.py:15
  15.9 0.0 collective-permute-start
  17.2 0.1 maximum_bitcast_fusion
  17.3 0.1 select_reduce_fusion
  17.4 24.9 %collective-permute-done.1 = bf16[1,8,16,3,1536]{4,2,3,1,0:T(8,128)(2,1)S(1)} collective-permute-done((bf16[1,8,16,3,1536]{4,2,3,1,0:T(8,128)(2,1)S(1)}, bf16[1,8,16,3,1536]{4,2,3,1,0:T(8,128)(2,1)S(1)}, u32[]{:S(2)}, u32[]{:S(2)}) %collective-permute-start.1) | collective-permute-done | bytes 1179680 | tf_op jit(solution)/shard_map/ppermute | solution.py:15
  42.3 25.1 %collective-permute-done = bf16[1,8,16,3,1536]{4,2,3,1,0:T(8,128)(2,1)S(1)} collective-permute-done((bf16[1,8,16,3,1536]{4,2,3,1,0:T(8,128)(2,1)S(1)}, bf16[1,8,16,3,1536]{4,2,3,1,0:T(8,128)(2,1)S(1)}, u32[]{:S(2)}, u32[]{:S(2)}) %collective-permute-start) | collective-permute-done | bytes 1179680 | tf_op jit(solution)/shard_map/ppermute | solution.py:14
  67.4 0.4 pad_maximum_fusion
  67.8 5.4 %copy.25 = bf16[1,24,16,3,1536]{4,3,2,1,0:T(4,128)(2,1)} copy(bf16[1,24,16,3,1536]{4,2,3,1,0:T(8,128)(2,1)S(1)} %pad_maximum_fusion) | data formatting | bytes 7077888 | tf_op jit(solution)/shard_map/concatenate | solution.py:16
  73.2 6.2 %reshape.136 = bf16[24,73728]{1,0:T(8,128)(2,1)S(1)} reshape(bf16[1,24,16,3,1536]{4,3,2,1,0:T(4,128)(2,1)} %copy.25) | data formatting | bytes 7077888 | tf_op jit(solution)/shard_map/reshape | solution.py:56
  79.4 6.2 %dot_general.8 = bf16[16,3,1536,24]{2,1,0,3:T(4,128)(2,1)} reshape(bf16[73728,24]{0,1:T(8,128)(2,1)S(1)} %bitcast.25) | data formatting | bytes 7077888 | tf_op jit(solution)/shard_map/dot_general | solution.py:54
  85.6 8.3 %fusion = f32[8,16,3,1536]{3,0,2,1:T(8,128)} fusion(bf16[16,3,1536,24]{2,1,0,3:T(4,128)(2,1)} %dot_general.8, bf16[8,24]{1,0:T(8,128)(2,1)S(1)} %select_reduce_fusion), kind=kOutput, calls=%fused_computation.1 | convolution fusion | flops 28311552 | bytes 5898624 | tf_op jit(solution)/shard_map/dot_general | solution.py:54
  93.8 0.0 copy-start.2
  93.8 0.0 all-reduce.2.cloned.1.call-update
  93.9 67.2 %all-reduce.2.cloned.1.call-done = f32[8,16,3,1536]{3,0,2,1:T(8,128)} async-done(((f32[8,16,3,1536]{3,0,2,1:T(8,128)}), f32[8,16,3,1536]{3,0,2,1:T(8,128)}) %all-reduce.2.cloned.1.call-update) | async-done | bytes 2359312 | tf_op jit(solution)/shard_map/psum | solution.py:60
  161.0 0.0 copy-done.2
  161.0 0.0 copy-start
  161.0 1.4 slice_bitcast_fusion
  162.5 0.4 copy-done
  162.9 0.2 fusion.2
  163.1 1.5 copy.27
  164.6 1.3 copy.28
  (3 shorter events, 0.0 us)
Async XLA Ops:
  7.2 4.0 %copy-start.3 = (f32[1,1536]{1,0:T(1,128)S(1)}, f32[1,1536]{1,0:T(1,128)}, u32[]{:S(2)}) copy-start(f32[1,1536]{1,0:T(1,128)} %param.14) | copy-start | bytes 18436
  7.2 4.0 %copy-start.1 = (s32[1,8,16,1536]{3,2,1,0:T(8,128)S(1)}, s32[1,8,16,1536]{3,2,1,0:T(8,128)}, u32[]{:S(2)}) copy-start(s32[1,8,16,1536]{3,2,1,0:T(8,128)} %param.9) | copy-start | bytes 2359300
  7.2 4.0 %copy-start.4 = (s32[1,8]{1,0:T(1,128)S(1)}, s32[1,8]{1,0:T(1,128)}, u32[]{:S(2)}) copy-start(s32[1,8]{1,0:T(1,128)} %param.10) | copy-start | bytes 100
  7.2 153.8 %all-reduce.2.cloned.1.call-start = ((), (), s32[]{:S(2)}) async-start(), calls=%async_computation | async-start | bytes 4718592 | tf_op jit(solution)/shard_map/psum | solution.py:60
  11.9 30.3 %collective-permute-start.1 = (bf16[1,8,16,3,1536]{4,2,3,1,0:T(8,128)(2,1)S(1)}, bf16[1,8,16,3,1536]{4,2,3,1,0:T(8,128)(2,1)S(1)}, u32[]{:S(2)}, u32[]{:S(2)}) collective-permute-start(bf16[1,8,16,3,1536]{4,2,3,1,0:T(8,128)(2,1)S(1)} %pad_maximum_fusion.1), channel_id=1, source_target_pairs={{8,0},{16,8},{24,16},{0,24},{9,1},{17,9},{25,17},{1,25},{10,2},{18... | collective-permute-start | bytes 3538952 | tf_op jit(solution)/shard_map/ppermute | solution.py:15
  15.9 51.5 %collective-permute-start = (bf16[1,8,16,3,1536]{4,2,3,1,0:T(8,128)(2,1)S(1)}, bf16[1,8,16,3,1536]{4,2,3,1,0:T(8,128)(2,1)S(1)}, u32[]{:S(2)}, u32[]{:S(2)}) collective-permute-start(bf16[1,8,16,3,1536]{4,2,3,1,0:T(8,128)(2,1)S(1)} %pad_maximum_fusion.1), channel_id=1, source_target_pairs={{0,8},{8,16},{16,24},{24,0},{1,9},{9,17},{17,25},{25,1},{2,10},{10... | collective-permute-start | bytes 3538952 | tf_op jit(solution)/shard_map/ppermute | solution.py:14
  93.8 67.2 %copy-start.2 = (f32[1536]{0:T(1024)S(1)}, f32[1536]{0:T(1024)}, u32[]{:S(2)}) copy-start(f32[1536]{0:T(1024)} %param.15) | copy-start | bytes 18436
  161.0 1.9 %copy-start = (f32[8,16,3,1536]{3,0,2,1:T(8,128)S(1)}, f32[8,16,3,1536]{3,0,2,1:T(8,128)}, u32[]{:S(2)}) copy-start(f32[8,16,3,1536]{3,0,2,1:T(8,128)} %all-reduce.2.cloned.1.call-done) | copy-start | bytes 7077892
Sparse Core Ops, SparseCore 0:
  94.0 67.0 all-reduce.1
where the time goes:
time: 173 us
  waiting for transfers between devices  117 us (68%)
  local copies, waits for them, and re-layouts  24.9 us (14%)
  between operations  15.5 us (9%)
  matrix products  8.26 us (5%)
  starting transfers between devices  3.99 us (2%)
  other arithmetic  2.95 us (2%)
    psum x1, waiting for transfers between devices, shards(): totals = lax.psum(partial_numerator, 'night')  67.2 us
    ppermute x1, waiting for transfers between devices, extended(): before = lax.ppermute(last, axis, up)  25.1 us
    ppermute x1, waiting for transfers between devices, extended(): after = lax.ppermute(first, axis, down)  24.9 us
    dot_general x1, matrix products, shards(): jnp.dot(matrix.reshape(sample_count, local_nights * 3 * sample_count), pa...  8.26 us
    dot_general x1, local copies, waits for them, and re-layouts, shards(): jnp.dot(matrix.reshape(sample_count, local_nights * 3 * sample_count), pa...  6.2 us
    reshape x1, local copies, waits for them, and re-layouts, shards(): padded_slab.reshape(local_nights * 3 * sample_count, baseline_count * 3 *...  6.2 us
    concatenate x1, local copies, waits for them, and re-layouts, extended(): x = jnp.concatenate([before, x, after], axis=dim)  5.36 us
    ppermute x1, starting transfers between devices, extended(): after = lax.ppermute(first, axis, down)  3.95 us
  transfers between devices with their start and end apart: 3, of which 3 were waited for; matrix products, arithmetic and copies ran while one was open for 0% of the time, Pallas kernels for 0%

commit v1 on v0

--- a/solution.py
+++ b/solution.py
@@ -57,7 +57,9 @@
         preferred_element_type=jnp.float32,
     )
     partial_numerator = partial_numerator.reshape(sample_count, baseline_count, 3, channel_count)
-    totals = lax.psum(partial_numerator, "night")
+    totals = partial_numerator
+    for hop in (1, 2, 4):
+        totals = totals + lax.ppermute(totals, "night", [(dev, dev ^ hop) for dev in range(8)])
     denominator_sum = totals[:, :, 2]
     binned = (
         totals[:, :, 0:2] / (denominator_sum[:, :, None, :] + prior[None, None, None, :])

time: 173 us -> 252 us (1.46)
  waiting for transfers between devices: 117 us -> 208 us
  between operations: 15.5 us -> 2.13 us
  starting transfers between devices: 3.99 us -> 8.26 us
    ppermute x0 -> x3, waiting for transfers between devices: none -> 158 us  [shards(): lax.ppermute(totals, 'night', [(dev, dev ^ hop) for dev in range(8)])]
    psum x1 -> x0, waiting for transfers between devices: 67.2 us -> none  [shards(): totals = lax.psum(partial_numerator, 'night')]
    ppermute x0 -> x3, starting transfers between devices: none -> 4.32 us  [shards(): lax.ppermute(totals, 'night', [(dev, dev ^ hop) for dev in range(8)])]
  transfers between devices with their start and end apart: 3 -> 5, of which waited for: 3 -> 5; matrix products, arithmetic and copies ran while one was open for 0% -> 0% of each run, Pallas kernels for 0% -> 0%
where the time goes in v1:
time: 252 us
  waiting for transfers between devices  208 us (83%)
  local copies, waits for them, and re-layouts  24.5 us (10%)
  starting transfers between devices  8.26 us (3%)
  matrix products  6.82 us (3%)
  other arithmetic  2.83 us (1%)
    ppermute x3, waiting for transfers between devices, shards(): lax.ppermute(totals, 'night', [(dev, dev ^ hop) for dev in range(8)])  158 us
    ppermute x1, waiting for transfers between devices, extended(): before = lax.ppermute(last, axis, up)  25.1 us
    ppermute x1, waiting for transfers between devices, extended(): after = lax.ppermute(first, axis, down)  24.9 us
    dot_general x1, matrix products, shards(): jnp.dot(matrix.reshape(sample_count, local_nights * 3 * sample_count), pa...  6.82 us
    reshape x1, local copies, waits for them, and re-layouts, shards(): padded_slab.reshape(local_nights * 3 * sample_count, baseline_count * 3 *...  6.2 us
    dot_general x1, local copies, waits for them, and re-layouts, shards(): jnp.dot(matrix.reshape(sample_count, local_nights * 3 * sample_count), pa...  6.2 us
    concatenate x1, local copies, waits for them, and re-layouts, extended(): x = jnp.concatenate([before, x, after], axis=dim)  5.36 us
  transfers between devices with their start and end apart: 5, of which 5 were waited for; matrix products, arithmetic and copies ran while one was open for 0% of the time, Pallas kernels for 0%

profile of v1, /device:TPU:0, one launch (start us, length us, event | category | flops | bytes accessed | tf_op | source)
XLA Modules:
  0.0 252.1 jit_solution(7254685533747229039)
XLA Ops:
  0.6 0.0 copy-start.2
  0.6 0.0 copy-start
  0.7 0.0 copy-start.3
  0.7 0.8 slice_reduce_fusion.1
  1.5 3.0 %fusion.11 = (bf16[1,8,16,1,1536]{4,3,2,1,0:T(2,128)(2,1)S(1)}, bf16[1,8,16,1,1536]{4,3,2,1,0:T(2,128)(2,1)S(1)}) fusion(bf16[1,8,16,2,1536]{4,3,2,1,0:T(2,128)(2,1)} %param.8), kind=kLoop, calls=%fused_computation.29 | loop fusion | bytes 1572864 | tf_op jit(solution)/shard_map/slice | solution.py:37
  4.5 0.0 copy-done.2
  4.6 0.0 copy-done
  4.6 0.0 copy-done.3
  4.6 0.2 fusion.7
  4.8 0.3 fusion.4
  5.1 0.1 fusion.3
  5.2 0.1 pad_maximum_fusion.1
  5.3 3.9 %collective-permute-start.1 = (bf16[1,8,16,3,1536]{4,2,3,1,0:T(8,128)(2,1)S(1)}, bf16[1,8,16,3,1536]{4,2,3,1,0:T(8,128)(2,1)S(1)}, u32[]{:S(2)}, u32[]{:S(2)}) collective-permute-start(bf16[1,8,16,3,1536]{4,2,3,1,0:T(8,128)(2,1)S(1)} %pad_maximum_fusion.1), channel_id=1, source_target_pairs={{8,0},{16,8},{24,16},{0,24},{9,1},{17,9},{25,17},{1,25},{10,2},{18... | collective-permute-start | bytes 3538952 | tf_op jit(solution)/shard_map/ppermute | solution.py:15
  9.3 0.0 collective-permute-start
  10.6 0.1 maximum_bitcast_fusion
  10.7 0.1 select_reduce_fusion
  10.8 24.9 %collective-permute-done.1 = bf16[1,8,16,3,1536]{4,2,3,1,0:T(8,128)(2,1)S(1)} collective-permute-done((bf16[1,8,16,3,1536]{4,2,3,1,0:T(8,128)(2,1)S(1)}, bf16[1,8,16,3,1536]{4,2,3,1,0:T(8,128)(2,1)S(1)}, u32[]{:S(2)}, u32[]{:S(2)}) %collective-permute-start.1) | collective-permute-done | bytes 1179680 | tf_op jit(solution)/shard_map/ppermute | solution.py:15
  35.7 25.1 %collective-permute-done = bf16[1,8,16,3,1536]{4,2,3,1,0:T(8,128)(2,1)S(1)} collective-permute-done((bf16[1,8,16,3,1536]{4,2,3,1,0:T(8,128)(2,1)S(1)}, bf16[1,8,16,3,1536]{4,2,3,1,0:T(8,128)(2,1)S(1)}, u32[]{:S(2)}, u32[]{:S(2)}) %collective-permute-start) | collective-permute-done | bytes 1179680 | tf_op jit(solution)/shard_map/ppermute | solution.py:14
  60.8 0.4 pad_maximum_fusion
  61.2 5.4 %copy.25 = bf16[1,24,16,3,1536]{4,3,2,1,0:T(4,128)(2,1)} copy(bf16[1,24,16,3,1536]{4,2,3,1,0:T(8,128)(2,1)S(1)} %pad_maximum_fusion) | data formatting | bytes 7077888 | tf_op jit(solution)/shard_map/concatenate | solution.py:16
  66.6 6.2 %reshape.136 = bf16[24,73728]{1,0:T(8,128)(2,1)S(1)} reshape(bf16[1,24,16,3,1536]{4,3,2,1,0:T(4,128)(2,1)} %copy.25) | data formatting | bytes 7077888 | tf_op jit(solution)/shard_map/reshape | solution.py:56
  72.8 6.2 %dot_general.8 = bf16[16,3,1536,24]{2,1,0,3:T(4,128)(2,1)} reshape(bf16[73728,24]{0,1:T(8,128)(2,1)S(1)} %bitcast.25) | data formatting | bytes 7077888 | tf_op jit(solution)/shard_map/dot_general | solution.py:54
  79.0 6.8 %fusion = f32[8,16,3,1536]{3,0,2,1:T(8,128)S(1)} fusion(bf16[16,3,1536,24]{2,1,0,3:T(4,128)(2,1)} %dot_general.8, bf16[8,24]{1,0:T(8,128)(2,1)S(1)} %select_reduce_fusion), kind=kOutput, calls=%fused_computation.1 | convolution fusion | flops 28311552 | bytes 5898624 | tf_op jit(solution)/shard_map/dot_general | solution.py:54
  85.8 0.0 collective-permute-start.2
  85.8 4.5 %collective-permute-done.2 = f32[8,16,3,1536]{3,0,2,1:T(8,128)S(1)} collective-permute-done((f32[8,16,3,1536]{3,0,2,1:T(8,128)S(1)}, f32[8,16,3,1536]{3,0,2,1:T(8,128)S(1)}, u32[]{:S(2)}, u32[]{:S(2)}) %collective-permute-start.2) | collective-permute-done | bytes 2359328 | tf_op jit(solution)/shard_map/ppermute | solution.py:62
  90.3 0.4 add.79
  90.7 1.6 collective-permute-start.3
  92.4 51.7 %collective-permute-done.3 = f32[8,16,3,1536]{3,0,2,1:T(8,128)S(1)} collective-permute-done((f32[8,16,3,1536]{3,0,2,1:T(8,128)S(1)}, f32[8,16,3,1536]{3,0,2,1:T(8,128)S(1)}, u32[]{:S(2)}, u32[]{:S(2)}) %collective-permute-start.3) | collective-permute-done | bytes 2359328 | tf_op jit(solution)/shard_map/ppermute | solution.py:62
  144.1 0.4 add.80
  144.5 0.0 copy-start.1
  144.5 2.7 %collective-permute-start.4 = (f32[8,16,3,1536]{3,0,2,1:T(8,128)S(1)}, f32[8,16,3,1536]{3,0,2,1:T(8,128)S(1)}, u32[]{:S(2)}, u32[]{:S(2)}) collective-permute-start(f32[8,16,3,1536]{3,0,2,1:T(8,128)S(1)} %add.80), channel_id=1, source_target_pairs={{0,4},{1,5},{2,6},{3,7},{4,0},{5,1},{6,2},{7,3},{8,12},{9,13},{10,... | collective-permute-start | bytes 7077896 | tf_op jit(solution)/shard_map/ppermute | solution.py:62
  147.1 101.3 %collective-permute-done.4 = f32[8,16,3,1536]{3,0,2,1:T(8,128)S(1)} collective-permute-done((f32[8,16,3,1536]{3,0,2,1:T(8,128)S(1)}, f32[8,16,3,1536]{3,0,2,1:T(8,128)S(1)}, u32[]{:S(2)}, u32[]{:S(2)}) %collective-permute-start.4) | collective-permute-done | bytes 2359328 | tf_op jit(solution)/shard_map/ppermute | solution.py:62
  248.5 0.4 add.81
  248.8 0.0 copy-done.1
  248.8 0.2 slice_bitcast_fusion
  249.0 0.2 fusion.2
  249.2 1.5 copy.27
  250.7 1.3 copy.28
  (3 shorter events, 0.0 us)
Async XLA Ops:
  0.6 3.9 %copy-start.2 = (f32[1,1536]{1,0:T(1,128)S(1)}, f32[1,1536]{1,0:T(1,128)}, u32[]{:S(2)}) copy-start(f32[1,1536]{1,0:T(1,128)} %param.14) | copy-start | bytes 18436
  0.6 3.9 %copy-start = (s32[1,8,16,1536]{3,2,1,0:T(8,128)S(1)}, s32[1,8,16,1536]{3,2,1,0:T(8,128)}, u32[]{:S(2)}) copy-start(s32[1,8,16,1536]{3,2,1,0:T(8,128)} %param.9) | copy-start | bytes 2359300
  0.7 3.9 %copy-start.3 = (s32[1,8]{1,0:T(1,128)S(1)}, s32[1,8]{1,0:T(1,128)}, u32[]{:S(2)}) copy-start(s32[1,8]{1,0:T(1,128)} %param.10) | copy-start | bytes 100
  5.3 30.3 %collective-permute-start.1 = (bf16[1,8,16,3,1536]{4,2,3,1,0:T(8,128)(2,1)S(1)}, bf16[1,8,16,3,1536]{4,2,3,1,0:T(8,128)(2,1)S(1)}, u32[]{:S(2)}, u32[]{:S(2)}) collective-permute-start(bf16[1,8,16,3,1536]{4,2,3,1,0:T(8,128)(2,1)S(1)} %pad_maximum_fusion.1), channel_id=1, source_target_pairs={{8,0},{16,8},{24,16},{0,24},{9,1},{17,9},{25,17},{1,25},{10,2},{18... | collective-permute-start | bytes 3538952 | tf_op jit(solution)/shard_map/ppermute | solution.py:15
  9.3 51.5 %collective-permute-start = (bf16[1,8,16,3,1536]{4,2,3,1,0:T(8,128)(2,1)S(1)}, bf16[1,8,16,3,1536]{4,2,3,1,0:T(8,128)(2,1)S(1)}, u32[]{:S(2)}, u32[]{:S(2)}) collective-permute-start(bf16[1,8,16,3,1536]{4,2,3,1,0:T(8,128)(2,1)S(1)} %pad_maximum_fusion.1), channel_id=1, source_target_pairs={{0,8},{8,16},{16,24},{24,0},{1,9},{9,17},{17,25},{25,1},{2,10},{10... | collective-permute-start | bytes 3538952 | tf_op jit(solution)/shard_map/ppermute | solution.py:14
  85.8 4.5 %collective-permute-start.2 = (f32[8,16,3,1536]{3,0,2,1:T(8,128)S(1)}, f32[8,16,3,1536]{3,0,2,1:T(8,128)S(1)}, u32[]{:S(2)}, u32[]{:S(2)}) collective-permute-start(f32[8,16,3,1536]{3,0,2,1:T(8,128)S(1)} %fusion), channel_id=1, source_target_pairs={{0,1},{1,0},{2,3},{3,2},{4,5},{5,4},{6,7},{7,6},{8,9},{9,8},{10,11... | collective-permute-start | bytes 7077896 | tf_op jit(solution)/shard_map/ppermute | solution.py:62
  90.7 53.4 %collective-permute-start.3 = (f32[8,16,3,1536]{3,0,2,1:T(8,128)S(1)}, f32[8,16,3,1536]{3,0,2,1:T(8,128)S(1)}, u32[]{:S(2)}, u32[]{:S(2)}) collective-permute-start(f32[8,16,3,1536]{3,0,2,1:T(8,128)S(1)} %add.79), channel_id=1, source_target_pairs={{0,2},{1,3},{2,0},{3,1},{4,6},{5,7},{6,4},{7,5},{8,10},{9,11},{10,... | collective-permute-start | bytes 7077896 | tf_op jit(solution)/shard_map/ppermute | solution.py:62
  144.5 104.4 %copy-start.1 = (f32[1536]{0:T(1024)S(1)}, f32[1536]{0:T(1024)}, u32[]{:S(2)}) copy-start(f32[1536]{0:T(1024)} %param.15) | copy-start | bytes 18436
  144.5 104.0 %collective-permute-start.4 = (f32[8,16,3,1536]{3,0,2,1:T(8,128)S(1)}, f32[8,16,3,1536]{3,0,2,1:T(8,128)S(1)}, u32[]{:S(2)}, u32[]{:S(2)}) collective-permute-start(f32[8,16,3,1536]{3,0,2,1:T(8,128)S(1)} %add.80), channel_id=1, source_target_pairs={{0,4},{1,5},{2,6},{3,7},{4,0},{5,1},{6,2},{7,3},{8,12},{9,13},{10,... | collective-permute-start | bytes 7077896 | tf_op jit(solution)/shard_map/ppermute | solution.py:62
